TPU v7x, 32 devices: a whole 2x2x4 slice. The times are simulated.
32 devices in a mesh: cells: 16 (over z, x, core), nets: 2 (over y).
Axes of the slice: x: 2, y: 2, z: 4, core: 2. Of those that a mesh axis runs over, the one named last changes fastest.
Arguments:
- grad_out: bfloat16 [32768, 512], P(('cells', 'nets')), may hold values from -6 to 6
- saved_agg: bfloat16 [32768, 512], P(('cells', 'nets')), may hold values from -0.03125 to 0.03125
- theta: bfloat16 [512, 512], replicated, may hold values from -0.25 to 0.25
- tile_values: bfloat16 [16, 2, 16, 128, 128], P('cells', 'nets'), may hold values from -0.5 to 0.5
- tile_coords: int32 [16, 2, 16, 2], P('cells', 'nets'), may hold values from 0 to 15, as said below
- block_tile_count: int32 [16, 2], P('cells', 'nets'), may hold values from 4 to 16, as said below
- cell_degree: int32 [32768], P('cells'), may hold values from 1 to 8
- net_pin_count: int32 [2048], P('nets'), may hold values from 12 to 39
Outputs:
- grad_cells: bfloat16 [32768, 512], P(('cells', 'nets'))
- layer_weight_gradient: bfloat16 [512, 512], replicated
Inputs may be any that keep to these rules, and one draw needn't show every extreme that they name: `tile_coords`: within each block the 16 slots name distinct tiles: column 0 a cell tile below 16, column 1 a net tile below 8. Slots at and beyond the block's count carry no weight. `block_tile_count`: live slots of each block are its first ones; some block of every draw has all 16 live.
All inputs are finite; a program needn't handle non-finite values.
Results may differ from a plain program's by a relative error of at most 0.015.
Values may be sent and summed in bfloat16 or wider, within the bound.
A program may use at most 64 MiB of HBM per device.

v0:
```python
import jax
import jax.numpy as jnp
from jax import lax
from jax.sharding import PartitionSpec as P

TBLK = 16


def spread_nets(tile_vals, coords, live_mask, cell_tiles, net_count):
    tile_len = tile_vals.shape[-1]
    feature_dim = cell_tiles.shape[-1]
    running = jnp.zeros((net_count, tile_len, feature_dim), jnp.float32)
    selected_tiles = cell_tiles[coords[0:TBLK, 0]]
    matrix_product = jnp.einsum(
        "cnr,cnw->crw", tile_vals, selected_tiles, preferred_element_type=jnp.float32
    )
    weight = live_mask.astype(jnp.float32)[:, None, None]
    running = running.at[coords[0:TBLK, 1]].add(matrix_product * weight)
    return running


def spread_cells(tile_vals, coords, live_mask, net_tiles, number_of_cells):
    tile_len = tile_vals.shape[-1]
    feature_dim = net_tiles.shape[-1]
    running = jnp.zeros((number_of_cells, tile_len, feature_dim), jnp.float32)
    selected_tiles = net_tiles[coords[0:TBLK, 1]]
    matrix_product = jnp.einsum(
        "jaf,jfw->jaw", tile_vals, selected_tiles, preferred_element_type=jnp.float32
    )
    weight = live_mask.astype(jnp.float32)[:, None, None]
    running = running.at[coords[0:TBLK, 0]].add(matrix_product * weight)
    return running


def shards(
    grad_out,
    saved_agg,
    theta,
    tile_values,
    tile_coords,
    block_tile_count,
    cell_degree,
    net_pin_count,
):
    own_rows = grad_out.shape[0]
    feature_dim = grad_out.shape[1]
    net_position = lax.axis_index("nets")
    cell_position = lax.axis_index("cells")
    own_degree = lax.dynamic_slice_in_dim(cell_degree, net_position * own_rows, own_rows)
    own_root = jnp.sqrt(own_degree.astype(jnp.float32))[:, None]
    grad_z = lax.dot_general(
        grad_out, theta, (((1,), (1,)), ((), ())), preferred_element_type=jnp.float32
    )
    scaled = (grad_z / own_root).astype(jnp.bfloat16)
    gathered = lax.all_gather(scaled, "nets", axis=0, tiled=True)
    theta_term = lax.dot_general(
        saved_agg, grad_out, (((0,), (0,)), ((), ())), preferred_element_type=jnp.float32
    )
    layer_weight_gradient = lax.psum(theta_term, ("cells", "nets")).astype(jnp.bfloat16)
    tile_vals = tile_values[0, 0]
    coords = tile_coords[0, 0]
    live_mask = jnp.arange(tile_vals.shape[0], dtype=jnp.int32) < block_tile_count[0, 0]
    block_cells = gathered.shape[0]
    block_nets = net_pin_count.shape[0]
    tile_len = tile_vals.shape[-1]
    number_of_cells = block_cells // tile_len
    net_count = block_nets // tile_len
    cell_tiles = gathered.reshape(number_of_cells, tile_len, feature_dim)
    net_partial = spread_nets(tile_vals, coords, live_mask, cell_tiles, net_count).reshape(
        block_nets, feature_dim
    )
    net_share = lax.psum_scatter(net_partial, "cells", scatter_dimension=0, tiled=True)
    share_rows = net_share.shape[0]
    share_degree = lax.dynamic_slice_in_dim(net_pin_count, cell_position * share_rows, share_rows)
    gradient_share = (net_share / share_degree.astype(jnp.float32)[:, None]).astype(jnp.bfloat16)
    net_grad = lax.all_gather(gradient_share, "cells", axis=0, tiled=True)
    net_tiles = net_grad.reshape(net_count, tile_len, feature_dim)
    cell_partial = spread_cells(tile_vals, coords, live_mask, net_tiles, number_of_cells).reshape(
        block_cells, feature_dim
    )
    cell_total = lax.psum_scatter(
        cell_partial.astype(jnp.bfloat16), "nets", scatter_dimension=0, tiled=True
    ).astype(jnp.float32)
    grad_cells = (cell_total / own_root).astype(jnp.bfloat16)
    return (grad_cells, layer_weight_gradient)


def solution(mesh):
    in_specs = (
        P(("cells", "nets"), None),
        P(("cells", "nets"), None),
        P(),
        P("cells", "nets", None, None, None),
        P("cells", "nets", None, None),
        P("cells", "nets"),
        P("cells"),
        P("nets"),
    )
    out_specs = (P(("cells", "nets"), None), P())
    return jax.shard_map(shards, mesh=mesh, in_specs=in_specs, out_specs=out_specs, check_vma=False)
```

profile of v0, /device:TPU:0, one launch (start us, length us, event | category | flops | bytes accessed | tf_op | source)
XLA Modules:
  0.0 261.6 jit_solution(6665885873084212178)
XLA Ops:
  7.2 0.0 copy-start
  7.2 0.0 all-gather.3.cloned.1.call-start
  7.2 0.8 convert_sqrt_fusion
  8.0 0.4 copy-done
  8.4 0.0 copy-start.2
  8.4 2.8 %divide_convert_fusion.1 = bf16[1024,512]{1,0:T(8,128)(2,1)} fusion(bf16[1024,512]{1,0:T(8,128)(2,1)S(1)} %copy-done, bf16[512,512]{1,0:T(8,128)(2,1)} %param.10, f32[1024]{0:T(1024)S(1)} %convert_sqrt_fusion), kind=kOutput, calls=%fused_computation.7 | convolution fusion | flops 537919488 | bytes 2625536 | tf_op jit(solution)/shard_map/dot_general | solution.py:51
  11.2 0.0 all-gather.3.cloned.1.call-update
  11.2 0.0 reduce-scatter.3.cloned.1.call-start
  11.9 0.0 copy-done.2
  11.9 35.2 %all-gather.3.cloned.1.call-done = bf16[2048,512]{1,0:T(8,128)(2,1)} async-done(((bf16[1024,512]{1,0:T(8,128)(2,1)}), bf16[2048,512]{1,0:T(8,128)(2,1)}) %all-gather.3.cloned.1.call-update) | async-done | bytes 2097168 | tf_op jit(solution)/shard_map/all_gather | solution.py:55
  47.2 2.3 gather_fusion
  49.5 3.9 %multiply_bitcast_fusion.1 = f32[16,128,512]{1,2,0:T(8,128)} fusion(bf16[16,128,512]{2,1,0:T(8,128)(2,1)S(1)} %gather_fusion, f32[16]{0:T(128)S(1)} %compare_convert_fusion, bf16[1,1,16,128,128]{4,3,2,1,0:T(8,128)(2,1)} %param.11), kind=kOutput, calls=%fused_computation.5 | convolution fusion | flops 269484032 | bytes 6815808 | tf_op jit(solution)/shard_map/cnr,cnw->crw/dot_general | solution.py:14
  53.3 5.4 %copy.13 = f32[16,128,512]{2,1,0:T(8,128)} copy(f32[16,128,512]{1,2,0:T(8,128)} %multiply_bitcast_fusion.1) | data formatting | bytes 8388608 | tf_op jit(solution)/shard_map/mul | solution.py:18
  58.7 0.2 broadcast_in_dim.5
  59.0 6.2 %scatter_fusion = f32[8,128,512]{2,1,0:T(8,128)S(1)} fusion(f32[8,128,512]{2,1,0:T(8,128)S(1)} %broadcast_in_dim.5, s32[16]{0:T(128)S(1)} %get-tuple-element.2, f32[16,128,512]{2,1,0:T(8,128)} %copy.13), kind=kCustom, calls=%fused_computation.2 | custom fusion | flops 1048576 | bytes 12582976 | tf_op jit(solution)/shard_map/scatter-add | solution.py:18
  65.1 0.0 copy-start.1
  65.1 1.3 copy-done.1
  66.5 0.0 reduce-scatter.3.cloned.1.call-update
  66.5 0.0 all-gather.5.cloned.1.call-start
  66.5 0.8 dynamic-slice_convert_fusion
  67.3 60.8 %reduce-scatter.3.cloned.1.call-done = f32[64,512]{1,0:T(8,128)} async-done(((f32[1024,512]{1,0:T(8,128)}), f32[64,512]{1,0:T(8,128)}) %reduce-scatter.3.cloned.1.call-update) | async-done | bytes 131088 | tf_op jit(solution)/shard_map/reduce_scatter | solution.py:72
  128.2 1.6 divide_convert_fusion.2
  129.8 0.0 all-gather.5.cloned.1.call-update
  129.8 0.0 reduce-scatter.5.cloned.1.call-start
  129.9 38.3 %all-gather.5.cloned.1.call-done = bf16[1024,512]{1,0:T(8,128)(2,1)} async-done(((bf16[64,512]{1,0:T(8,128)(2,1)}), bf16[1024,512]{1,0:T(8,128)(2,1)}) %all-gather.5.cloned.1.call-update) | async-done | bytes 1048592 | tf_op jit(solution)/shard_map/all_gather | solution.py:76
  168.2 1.9 gather_fusion.1
  170.1 3.9 %multiply_bitcast_fusion = f32[16,128,512]{1,2,0:T(8,128)} fusion(bf16[16,128,512]{2,1,0:T(8,128)(2,1)S(1)} %gather_fusion.1, f32[16]{0:T(128)S(1)} %compare_convert_fusion, bf16[1,1,16,128,128]{4,3,2,1,0:T(8,128)(2,1)} %param.11), kind=kOutput, calls=%fused_computation.4 | convolution fusion | flops 269484032 | bytes 6815808 | tf_op jit(solution)/shard_map/jaf,jfw->jaw/dot_general | solution.py:27
  174.0 5.3 %copy.15 = f32[16,128,512]{2,1,0:T(8,128)} copy(f32[16,128,512]{1,2,0:T(8,128)} %multiply_bitcast_fusion) | data formatting | bytes 8388608 | tf_op jit(solution)/shard_map/mul | solution.py:31
  179.3 2.5 broadcast_in_dim.4
  181.8 9.3 %scatter_fusion.1 = f32[16,128,512]{2,1,0:T(8,128)} fusion(f32[16,128,512]{2,1,0:T(8,128)} %broadcast_in_dim.4, s32[16]{0:T(128)S(1)} %get-tuple-element.3, f32[16,128,512]{2,1,0:T(8,128)} %copy.15), kind=kCustom, calls=%fused_computation.3 | custom fusion | flops 1048576 | bytes 12582976 | tf_op jit(solution)/shard_map/scatter-add | solution.py:31
  191.2 3.8 %convert_element_type.40 = bf16[16,128,512]{2,1,0:T(8,128)(2,1)} convert(f32[16,128,512]{2,1,0:T(8,128)} %scatter_fusion.1) | non-fusion elementwise | flops 1048576 | bytes 6291456 | tf_op jit(solution)/shard_map/convert_element_type | solution.py:82
  195.0 0.0 copy-start.3
  195.0 0.0 reduce-scatter.5.cloned.1.call-update
  195.0 1.2 copy-done.3
  196.2 0.7 fusion.4
  197.0 55.6 %all-reduce.1 = bf16[512,512]{1,0:T(8,128)(2,1)} all-reduce(f32[512,512]{1,0:T(8,128)S(1)} %fusion.4), channel_id=1, replica_groups=mesh['cells'=16,'nets'=2] {'cells','nets'}, use_global_device_ids=true, to_apply=%region_4.0 | all-reduce | flops 262144 | bytes 1572864 | tf_op jit(solution)/shard_map/psum | solution.py:59
  252.6 0.0 reduce-scatter.5.cloned.1.call-done
  252.6 2.5 divide_convert_fusion
  (4 shorter events, 0.0 us)
Async XLA Ops:
  7.2 1.2 copy-start
  7.2 40.0 %all-gather.3.cloned.1.call-start = ((), (), s32[]{:S(2)}) async-start(), calls=%async_computation.2 | async-start | bytes 3145728 | tf_op jit(solution)/shard_map/all_gather | solution.py:55
  8.4 3.5 %copy-start.2 = (s32[1,1,16,2]{2,3,1,0:T(2,128)S(1)}, s32[1,1,16,2]{2,3,1,0:T(2,128)}, u32[]{:S(2)}) copy-start(s32[1,1,16,2]{2,3,1,0:T(2,128)} %param.12) | copy-start | bytes 388
  11.2 117.0 %reduce-scatter.3.cloned.1.call-start = ((), (), s32[]{:S(2)}) async-start(), calls=%async_computation.3 | async-start | bytes 2228224 | tf_op jit(solution)/shard_map/reduce_scatter | solution.py:72
  65.1 1.3 copy-start.1
  66.5 101.7 %all-gather.5.cloned.1.call-start = ((), (), s32[]{:S(2)}) async-start(), calls=%async_computation.4 | async-start | bytes 1114112 | tf_op jit(solution)/shard_map/all_gather | solution.py:76
  129.8 122.8 %reduce-scatter.5.cloned.1.call-start = ((), (), s32[]{:S(2)}) async-start(), calls=%async_computation.5 | async-start | bytes 3145728 | tf_op jit(solution)/shard_map/reduce_scatter | solution.py:81
  195.0 1.2 copy-start.3
Sparse Core Ops, SparseCore 0:
  11.3 35.8 all-gather.2
  66.6 61.4 reduce-scatter.2
  131.1 36.9 all-gather.4
  195.1 36.3 reduce-scatter.4
where the time goes:
time: 262 us
  waiting for transfers between devices  134 us (51%)
  blocking collectives  55.6 us (21%)
  other arithmetic  25 us (10%)
  local copies, waits for them, and re-layouts  20.6 us (8%)
  between operations  14.5 us (6%)
  matrix products  11.3 us (4%)
    reduce_scatter x1, waiting for transfers between devices, shards(): lax.psum_scatter(net_partial, 'cells', scatter_dimension=0, tiled=True)  60.8 us
    psum x1, blocking collectives, shards(): lax.psum(theta_term, ('cells', 'nets')).astype(jnp.bfloat16)  55.6 us
    all_gather x1, waiting for transfers between devices, shards(): net_grad = lax.all_gather(gradient_share, 'cells', axis=0, tiled=True)  38.3 us
    all_gather x1, waiting for transfers between devices, shards(): gathered = lax.all_gather(scaled, 'nets', axis=0, tiled=True)  35.2 us
    scatter-add x1, other arithmetic, spread_cells(): running = running.at[coords[0:TBLK, 0]].add(matrix_product * weight)  9.34 us
    scatter-add x1, other arithmetic, spread_nets(): running = running.at[coords[0:TBLK, 1]].add(matrix_product * weight)  6.16 us
    mul x1, local copies, waits for them, and re-layouts, spread_nets(): running = running.at[coords[0:TBLK, 1]].add(matrix_product * weight)  5.36 us
    mul x1, local copies, waits for them, and re-layouts, spread_cells(): running = running.at[coords[0:TBLK, 0]].add(matrix_product * weight)  5.34 us
  transfers between devices with their start and end apart: 4, of which 3 were waited for; matrix products, arithmetic and copies ran while one was open for 1% of the time, Pallas kernels for 0%

commit v1 on v0

--- a/solution.py
+++ b/solution.py
@@ -1,9 +1,17 @@
+import functools
+
 import jax
 import jax.numpy as jnp
 from jax import lax
+from jax.experimental import pallas as pl
+from jax.experimental.pallas import tpu as pltpu
 from jax.sharding import PartitionSpec as P
 
 TBLK = 16
+CHUNKS = 2
+F32 = jnp.float32
+BF16 = jnp.bfloat16
+MESH = pl.DeviceIdType.MESH
 
 
 def spread_nets(tile_vals, coords, live_mask, cell_tiles, net_count):
@@ -85,6 +93,359 @@
     return (grad_cells, layer_weight_gradient)
 
 
+def exchange_kernel(
+    grad_out, saved_agg, theta, tile_values, inv_vec, inv_own, degree, pins,
+    out_cells, out_weight,
+    go, sa, th, tiles_own, tiles_far, inv_land, inv_far, inc, scaled,
+    part, part_core, part_x, part_y, part_z, grads,
+    wpart, wpart_core, wpart_x, wpart_y, wpart_z, wgrads,
+    local_sem, send_sem, recv_sem,
+):
+    cell = lax.axis_index("cells")
+    y = lax.axis_index("nets")
+    z, x, core = cell // 4, (cell // 2) % 2, cell % 2
+
+    def device(zt, xt, ct, yt):
+        return ((zt * 2 + xt) * 2 + ct, yt)
+
+    to_core = device(z, x, 1 - core, y)
+    to_x = device(z, 1 - x, core, y)
+    to_y = device(z, x, core, 1 - y)
+    z_of = [lax.rem(z + d, 4) for d in range(4)]
+    to_z = [device(z_of[d], x, core, y) for d in range(4)]
+
+    loads = [
+        pltpu.make_async_copy(src, dst, local_sem.at[i])
+        for i, (src, dst) in enumerate(
+            ((theta, th), (grad_out, go), (tile_values.at[0, 0], tiles_own.at[pl.ds(0, 16)]), (saved_agg, sa))
+        )
+    ]
+    for load in loads:
+        load.start()
+
+    barrier = pltpu.get_barrier_semaphore()
+    partners = [to_core, to_x, to_y, to_z[1], to_z[2], to_z[3]]
+    for partner in partners:
+        pl.semaphore_signal(barrier, inc=1, device_id=partner, device_id_type=MESH)
+    pl.semaphore_wait(barrier, len(partners))
+
+    copies = []
+
+    def send(src, dst, target):
+        i = len(copies)
+        copy = pltpu.make_async_remote_copy(
+            src_ref=src, dst_ref=dst, send_sem=send_sem.at[i], recv_sem=recv_sem.at[i],
+            device_id=target, device_id_type=MESH,
+        )
+        copy.start()
+        copies.append(copy)
+        return copy
+
+    inv_copy = send(inv_vec, inv_land, to_y)
+    tile_copy = send(tile_values.at[0, 0], tiles_far.at[pl.ds(0, 16)], to_y)
+
+    tile_len = tiles_own.shape[-1]
+    zero_tile = jnp.zeros((tile_len, tile_len), BF16)
+    tiles_own[16] = zero_tile
+    tiles_far[16] = zero_tile
+
+    def dense(tiles, inv, block):
+        def row(r, carry):
+            for j in range(8):
+                slot = inv[0, (y * 8 + r) * 8 + j]
+                inc[
+                    block * 4 + j // 2,
+                    pl.ds(pl.multiple_of(r * tile_len, tile_len), tile_len),
+                    (j % 2) * tile_len : (j % 2 + 1) * tile_len,
+                ] = tiles[slot]
+            return carry
+
+        lax.fori_loop(0, 8, row, 0)
+
+    half = scaled.shape[1]
+    row_len = part.shape[3]
+
+    def net_part(h, block, xt):
+        def pair(p, carry):
+            j = block * 4 + xt * 2 + p
+            product = jnp.dot(scaled[h], inc[j], preferred_element_type=F32).astype(BF16)
+            for q in range(CHUNKS):
+                for s in range(2):
+                    part[q, h, j * 2 + s] = product[
+                        q * row_len : (q + 1) * row_len, s * tile_len : (s + 1) * tile_len
+                    ]
+            return carry
+
+        lax.fori_loop(0, 2, pair, 0)
+
+    def add(a, b):
+        return (a.astype(F32) + b.astype(F32)).astype(BF16)
+
+    def piece(block, xt):
+        return pl.ds(block * 8 + xt * 4, 4)
+
+    main = [
+        (part.at[q], part_core.at[q], part_x.at[q], part_y.at[q], part_z.at[q], grads.at[q])
+        for q in range(CHUNKS)
+    ]
+    weight = (wpart, wpart_core, wpart_x, wpart_y, wpart_z, wgrads)
+
+    def core_send(st, block, xt):
+        return send(st[0].at[1 - core, piece(block, xt)], st[1].at[piece(block, xt)], to_core)
+
+    def core_add(st, copy, block, xt):
+        copy.wait_recv()
+        at = piece(block, xt)
+        st[0][core, at] = add(st[0][core, at], st[1][at])
+
+    def x_send(st, block):
+        return send(st[0].at[core, piece(block, 1 - x)], st[2].at[block], to_x)
+
+    def x_add(st, copy, block):
+        copy.wait_recv()
+        at = piece(block, x)
+        st[0][core, at] = add(st[0][core, at], st[2][block])
+
+    def y_send(st):
+        return send(st[0].at[core, piece(1 - y, x)], st[3], to_y)
+
+    def y_add(st, copy):
+        copy.wait_recv()
+        at = piece(y, x)
+        st[0][core, at] = add(st[0][core, at], st[3][...])
+
+    mine = y * 8 + x * 4
+
+    def z_send(st):
+        return [send(st[0].at[core, mine + z_of[d]], st[4].at[d - 1], to_z[d]) for d in (1, 2, 3)]
+
+    def z_total(st, zs):
+        total = st[0][core, mine + z].astype(F32)
+        for d in (1, 2, 3):
+            zs[d - 1].wait_recv()
+            total = total + st[4][d - 1].astype(F32)
+        return total
+
+    def z_back(st):
+        at = st[5].at[core, mine + z]
+        return [send(at, at, to_z[d]) for d in (1, 2, 3)]
+
+    def forward(st, block, xt, target):
+        at = st[5].at[core, piece(block, xt)]
+        return send(at, at, target)
+
+    loads[0].wait()
+    loads[1].wait()
+    cells = go.shape[0]
+    root = jnp.sqrt(degree[0:1, pl.ds(pl.multiple_of(y * cells, cells), cells)].astype(F32))
+    for i in range(4):
+        n = cells // 4
+        for h in range(2):
+            z_rows = lax.dot_general(
+                th[h * half : (h + 1) * half], go[i * n : (i + 1) * n], (((1,), (1,)), ((), ())),
+                preferred_element_type=F32,
+            )
+            scaled[h, :, i * n : (i + 1) * n] = (z_rows / root[:, i * n : (i + 1) * n]).astype(BF16)
+
+    loads[2].wait()
+    dense(tiles_own, inv_own, y)
+    first = {}
+    for side in (0, 1):
+        xt = 1 - x if side == 0 else x
+        net_part(1 - core, y, xt)
+        first[side] = [core_send(st, y, xt) for st in main]
+        net_part(core, y, xt)
+    x_own = []
+    for q, st in enumerate(main):
+        core_add(st, first[0][q], y, 1 - x)
+        x_own.append(x_send(st, y))
+
+    loads[3].wait()
+    per = wpart.shape[2]
+
+    def weight_rows(i, carry):
+        rows = sa[:, pl.ds(pl.multiple_of(i * 128, 128), 128)]
+        term = lax.dot_general(rows, go[...], (((0,), (0,)), ((), ())), preferred_element_type=F32)
+        term = term.astype(BF16)
+        for j in range(128 // per):
+            wpart[i // 2, (i % 2) * (128 // per) + j] = term[j * per : (j + 1) * per]
+        return carry
+
+    lax.fori_loop(0, 4, weight_rows, 0)
+    w_core = {}
+    for block in (0, 1):
+        for side in (0, 1):
+            w_core[block, side] = core_send(weight, block, 1 - x if side == 0 else x)
+    for q, st in enumerate(main):
+        core_add(st, first[1][q], y, x)
+    w_x = []
+    for block in (0, 1):
+        core_add(weight, w_core[block, 0], block, 1 - x)
+        w_x.append(x_send(weight, block))
+    for block in (0, 1):
+        core_add(weight, w_core[block, 1], block, x)
+    for q, st in enumerate(main):
+        x_add(st, x_own[q], y)
+    for block in (0, 1):
+        x_add(weight, w_x[block], block)
+
+    inv_copy.wait_recv()
+    inv_move = pltpu.make_async_copy(inv_land, inv_far, local_sem.at[4])
+    inv_move.start()
+    inv_move.wait()
+    tile_copy.wait_recv()
+    w_y = y_send(weight)
+    dense(tiles_far, inv_far, 1 - y)
+    for side in (0, 1):
+        xt = 1 - x if side == 0 else x
+        net_part(1 - core, 1 - y, xt)
+        first[side] = [core_send(st, 1 - y, xt) for st in main]
+        net_part(core, 1 - y, xt)
+    x_far = []
+    for q, st in enumerate(main):
+        core_add(st, first[0][q], 1 - y, 1 - x)
+        x_far.append(x_send(st, 1 - y))
+    for q, st in enumerate(main):
+        core_add(st, first[1][q], 1 - y, x)
+    y_add(weight, w_y)
+    w_z = z_send(weight)
+    ys = []
+    for q, st in enumerate(main):
+        x_add(st, x_far[q], 1 - y)
+        ys.append(y_send(st))
+    weight[5][core, mine + z] = z_total(weight, w_z).astype(BF16)
+    w_zb = z_back(weight)
+    zs = []
+    for q, st in enumerate(main):
+        y_add(st, ys[q])
+        zs.append(z_send(st))
+    for copy in w_zb:
+        copy.wait_recv()
+    w_yb = forward(weight, y, x, to_y)
+    w_xb = [forward(weight, y, x, to_x)]
+    w_cb = [forward(weight, y, x, to_core)]
+    pin_row = pins[0:1, pl.ds(pl.multiple_of((x * 4 + z) * tile_len, tile_len), tile_len)].astype(F32)
+    zb = []
+    for q, st in enumerate(main):
+        st[5][core, mine + z] = (z_total(st, zs[q]) / pin_row).astype(BF16)
+        zb.append(z_back(st))
+    w_yb.wait_recv()
+    w_xb.append(forward(weight, 1 - y, x, to_x))
+    w_cb.append(forward(weight, 1 - y, x, to_core))
+    yb, xb, cb = [], [], []
+    for q, st in enumerate(main):
+        for copy in zb[q]:
+            copy.wait_recv()
+        yb.append(forward(st, y, x, to_y))
+        xb.append([forward(st, y, x, to_x)])
+        cb.append(forward(st, y, x, to_core))
+    for i in (0, 1):
+        w_xb[i].wait_recv()
+        w_cb.append(forward(weight, y if i == 0 else 1 - y, 1 - x, to_core))
+    for q, st in enumerate(main):
+        yb[q].wait_recv()
+        xb[q].append(forward(st, 1 - y, x, to_x))
+        cb.append(forward(st, 1 - y, x, to_core))
+    for copy in w_cb:
+        copy.wait_recv()
+    for t in range(32):
+        out_weight[t * per : (t + 1) * per, :] = wgrads[t // 16, t % 16]
+    for i in (0, 1):
+        for q, st in enumerate(main):
+            xb[q][i].wait_recv()
+            cb.append(forward(st, y if i == 0 else 1 - y, 1 - x, to_core))
+    for copy in cb:
+        copy.wait_recv()
+
+    def cell_rows(r, carry):
+        at = pl.ds(pl.multiple_of(r * 128, 128), 128)
+        root_row = jnp.sqrt(
+            degree[0:1, pl.ds(pl.multiple_of(y * cells + r * 128, 128), 128)].astype(F32)
+        )
+        root_tile = jnp.broadcast_to(root_row, (128, 128)).T
+        for h in range(2):
+            for q in range(CHUNKS):
+                total = jnp.zeros((128, row_len), F32)
+                for j in range(8):
+                    net_rows = jnp.concatenate([grads[q, h, 2 * j], grads[q, h, 2 * j + 1]], axis=1)
+                    total = total + lax.dot_general(
+                        inc[j, at, :], net_rows, (((1,), (1,)), ((), ())), preferred_element_type=F32
+                    )
+                at_col = h * half + q * row_len
+                out_cells[at, at_col : at_col + row_len] = (total / root_tile[:, :row_len]).astype(BF16)
+        return carry
+
+    lax.fori_loop(0, cells // 128, cell_rows, 0)
+    for copy in copies:
+        copy.wait_send()
+
+
+def fused_shards(
+    grad_out, saved_agg, theta, tile_values, tile_coords, block_tile_count, cell_degree, net_pin_count
+):
+    rows, width = grad_out.shape
+    slots, tile_len = tile_values.shape[2], tile_values.shape[3]
+    nets = net_pin_count.shape[0]
+    net_tiles = nets // tile_len
+    places = jnp.arange(128, dtype=jnp.int32)
+    coords = tile_coords[0, 0]
+    slot = jnp.arange(slots, dtype=jnp.int32)
+    code = jnp.where(slot < block_tile_count[0, 0], coords[:, 0] * net_tiles + coords[:, 1], -1)
+    found = code[:, None] == places[None, :]
+    inv = slots + jnp.sum(jnp.where(found, slot[:, None] - slots, 0), axis=0)
+    inv = jnp.broadcast_to(inv[None, :], (8, 128)).astype(jnp.int32)
+    half, row_len = width // 2, width // 2 // CHUNKS
+    per = width // 32
+    vmem = pltpu.VMEM
+    any_spec = pl.BlockSpec(memory_space=pl.ANY)
+    vmem_spec = pl.BlockSpec(memory_space=pltpu.VMEM)
+
+    def stage_buffers(lead, block):
+        return [
+            vmem(lead + (2, 16) + block, BF16),
+            vmem(lead + (16,) + block, BF16),
+            vmem(lead + (2, 4) + block, BF16),
+            vmem(lead + (4,) + block, BF16),
+            vmem(lead + (3,) + block, BF16),
+            vmem(lead + (2, 16) + block, BF16),
+        ]
+
+    return pl.pallas_call(
+        exchange_kernel,
+        out_shape=(
+            jax.ShapeDtypeStruct((rows, width), BF16),
+            jax.ShapeDtypeStruct((width, width), BF16),
+        ),
+        in_specs=[any_spec] * 4
+        + [vmem_spec, pl.BlockSpec(memory_space=pltpu.SMEM), vmem_spec, vmem_spec],
+        out_specs=(vmem_spec, vmem_spec),
+        scratch_shapes=[
+            vmem((rows, width), BF16),
+            vmem((rows, width), BF16),
+            vmem((width, width), BF16),
+            vmem((slots + 1, tile_len, tile_len), BF16),
+            vmem((slots + 1, tile_len, tile_len), BF16),
+            vmem((8, 128), jnp.int32),
+            pltpu.SMEM((8, 128), jnp.int32),
+            vmem((net_tiles, rows, 2 * tile_len), BF16),
+            vmem((2, half, rows), BF16),
+        ]
+        + stage_buffers((CHUNKS,), (row_len, tile_len))
+        + stage_buffers((), (per, width))
+        + [
+            pltpu.SemaphoreType.DMA((8,)),
+            pltpu.SemaphoreType.DMA((96,)),
+            pltpu.SemaphoreType.DMA((96,)),
+        ],
+        compiler_params=pltpu.CompilerParams(
+            collective_id=0, has_side_effects=True, vmem_limit_bytes=48 * 1024 * 1024
+        ),
+    )(
+        grad_out, saved_agg, theta, tile_values, inv, inv,
+        cell_degree.reshape(1, -1), net_pin_count.reshape(1, -1),
+    )
+
+
 def solution(mesh):
     in_specs = (
         P(("cells", "nets"), None),
@@ -96,5 +457,8 @@
         P("cells"),
         P("nets"),
     )
+    fused = mesh.shape["cells"] == 16 and mesh.shape["nets"] == 2
     out_specs = (P(("cells", "nets"), None), P())
-    return jax.shard_map(shards, mesh=mesh, in_specs=in_specs, out_specs=out_specs, check_vma=False)
+    return jax.shard_map(
+        fused_shards if fused else shards, mesh=mesh, in_specs=in_specs, out_specs=out_specs, check_vma=False,
+    )

time: 262 us -> 73.2 us (0.28)
  waiting for transfers between devices: 134 us -> 0 us
  Pallas kernels: 0 us -> 63 us
  blocking collectives: 55.6 us -> 0 us
  other arithmetic: 25 us -> 0.1 us
  between operations: 14.5 us -> 1.32 us
  local copies, waits for them, and re-layouts: 20.6 us -> 7.54 us
  matrix products: 11.3 us -> 0 us
    all_gather x2 -> x0, waiting for transfers between devices: 73.5 us -> none  [the longest x1 38.3 us: shards(): net_grad = lax.all_gather(gradient_share, 'cells', axis=0, tiled=True)]
    pallas_call x0 -> x1, Pallas kernels: none -> 63 us  [fused_shards(): pl.pallas_call(exchange_kernel, out_shape=(jax.ShapeDtypeStruct((rows, wi...]
    reduce_scatter x2 -> x0, waiting for transfers between devices: 60.8 us -> none  [the longest x1 60.8 us: shards(): lax.psum_scatter(net_partial, 'cells', scatter_dimension=0, tiled=True)]
    psum x1 -> x0, blocking collectives: 55.6 us -> none  [shards(): lax.psum(theta_term, ('cells', 'nets')).astype(jnp.bfloat16)]
    scatter-add x2 -> x0, other arithmetic: 15.5 us -> none  [the longest x1 9.34 us: spread_cells(): running = running.at[coords[0:TBLK, 0]].add(matrix_product * weight)]
    dot_general x4 -> x0, matrix products: 11.3 us -> none  [the longest x1 3.93 us: spread_cells(): jnp.einsum('jaf,jfw->jaw', tile_vals, selected_tiles, preferred_element_t...]
    mul x2 -> x0, local copies, waits for them, and re-layouts: 10.7 us -> none  [the longest x1 5.36 us: spread_nets(): running = running.at[coords[0:TBLK, 1]].add(matrix_product * weight)]
    convert_element_type x5 -> x0, other arithmetic: 8.69 us -> none  [the longest x1 3.81 us: shards(): cell_partial.astype(jnp.bfloat16)]
  transfers between devices with their start and end apart: 4 -> 0, of which waited for: 3 -> 0; matrix products, arithmetic and copies ran while one was open for 1% -> 0% of each run, Pallas kernels for 0% -> 0%
where the time goes in v1:
time: 73.2 us; the launch traced here: 72 us
  Pallas kernels  63 us (86%)
  local copies, waits for them, and re-layouts  7.54 us (10%)
  between operations  1.32 us (2%)
    pallas_call x1, Pallas kernels, fused_shards(): pl.pallas_call(exchange_kernel, out_shape=(jax.ShapeDtypeStruct((rows, wi...  63 us
    unnamed x16, local copies, waits for them, and re-layouts  7.54 us

profile of v1, /device:TPU:0, one launch (start us, length us, event | category | flops | bytes accessed | tf_op | source)
XLA Modules:
  0.0 72.0 jit_solution(802917341711006631)
XLA Ops:
  1.3 0.0 copy-start.6
  1.3 0.0 copy-start.4
  1.3 0.7 copy-done.6
  2.0 0.0 copy-start.5
  2.0 0.1 select_reduce_fusion
  2.1 0.0 copy-done.4
  2.1 0.6 copy-done.5
  2.7 0.0 copy-start
  2.7 1.2 %copy-done = bf16[1024,512]{1,0:T(8,128)(2,1)S(1)} copy-done((bf16[1024,512]{1,0:T(8,128)(2,1)S(1)}, bf16[1024,512]{1,0:T(8,128)(2,1)}, u32[]{:S(2)}) %copy-start) | copy-done | bytes 1048600
  3.9 0.0 copy-start.1
  3.9 1.2 %copy-done.1 = bf16[1024,512]{1,0:T(8,128)(2,1)S(1)} copy-done((bf16[1024,512]{1,0:T(8,128)(2,1)S(1)}, bf16[1024,512]{1,0:T(8,128)(2,1)}, u32[]{:S(2)}) %copy-start.1) | copy-done | bytes 1048600
  5.1 0.0 copy-start.2
  5.1 1.0 %copy-done.2 = bf16[512,512]{1,0:T(8,128)(2,1)S(1)} copy-done((bf16[512,512]{1,0:T(8,128)(2,1)S(1)}, bf16[512,512]{1,0:T(8,128)(2,1)}, u32[]{:S(2)}) %copy-start.2) | copy-done | bytes 524312
  6.1 0.0 copy-start.3
  6.1 1.0 %copy-done.3 = bf16[1,1,16,128,128]{4,3,2,1,0:T(8,128)(2,1)S(1)} copy-done((bf16[1,1,16,128,128]{4,3,2,1,0:T(8,128)(2,1)S(1)}, bf16[1,1,16,128,128]{4,3,2,1,0:T(8,128)(2,1)}, u32[]{:S(2)}) %copy-start.3) | copy-done | bytes 524312
  7.2 63.0 %shard_map.95 = (bf16[1024,512]{1,0:T(8,128)(2,1)S(1)}, bf16[512,512]{1,0:T(8,128)(2,1)S(1)}) custom-call(bf16[1024,512]{1,0:T(8,128)(2,1)S(1)} %copy-done, bf16[1024,512]{1,0:T(8,128)(2,1)S(1)} %copy-done.1, bf16[512,512]{1,0:T(8,128)(2,1)S(1)} %copy-done.2, bf16[1,1,16,128,128]{4,3,2,1,0:T(8,128)(2,1)S(1)} %copy-done.3, ...), custom_call_target="tpu_custom_call" | custom-call | tf_op jit(solution)/shard_map/pallas_call | solution.py:413
  70.2 1.0 %copy.13 = bf16[1024,512]{1,0:T(8,128)(2,1)} copy(bf16[1024,512]{1,0:T(8,128)(2,1)S(1)} %get-tuple-element.4) | data formatting | bytes 2097152
  71.2 0.8 %copy.14 = bf16[512,512]{1,0:T(8,128)(2,1)} copy(bf16[512,512]{1,0:T(8,128)(2,1)S(1)} %get-tuple-element.5) | data formatting | bytes 1048576
  (4 shorter events, 0.0 us)
Async XLA Ops:
  1.3 0.7 copy-start.6
  1.3 0.8 %copy-start.4 = (s32[2048]{0:T(1024)S(1)}, s32[2048]{0:T(1024)}, u32[]{:S(2)}) copy-start(s32[2048]{0:T(1024)} %param.14) | copy-start | bytes 24580
  2.0 0.7 copy-start.5
  2.7 1.2 %copy-start = (bf16[1024,512]{1,0:T(8,128)(2,1)S(1)}, bf16[1024,512]{1,0:T(8,128)(2,1)}, u32[]{:S(2)}) copy-start(bf16[1024,512]{1,0:T(8,128)(2,1)} %grad_out.1) | copy-start | bytes 3145732
  3.9 1.2 %copy-start.1 = (bf16[1024,512]{1,0:T(8,128)(2,1)S(1)}, bf16[1024,512]{1,0:T(8,128)(2,1)}, u32[]{:S(2)}) copy-start(bf16[1024,512]{1,0:T(8,128)(2,1)} %saved_agg.1) | copy-start | bytes 3145732
  5.1 1.0 %copy-start.2 = (bf16[512,512]{1,0:T(8,128)(2,1)S(1)}, bf16[512,512]{1,0:T(8,128)(2,1)}, u32[]{:S(2)}) copy-start(bf16[512,512]{1,0:T(8,128)(2,1)} %theta.1) | copy-start | bytes 1572868
  6.1 1.0 %copy-start.3 = (bf16[1,1,16,128,128]{4,3,2,1,0:T(8,128)(2,1)S(1)}, bf16[1,1,16,128,128]{4,3,2,1,0:T(8,128)(2,1)}, u32[]{:S(2)}) copy-start(bf16[1,1,16,128,128]{4,3,2,1,0:T(8,128)(2,1)} %tile_values.1) | copy-start | bytes 1572868

commit v2 on v1

--- a/solution.py
+++ b/solution.py
@@ -8,7 +8,7 @@
 from jax.sharding import PartitionSpec as P
 
 TBLK = 16
-CHUNKS = 2
+CHUNKS = 4
 F32 = jnp.float32
 BF16 = jnp.bfloat16
 MESH = pl.DeviceIdType.MESH
@@ -94,9 +94,9 @@
 
 
 def exchange_kernel(
-    grad_out, saved_agg, theta, tile_values, inv_vec, inv_own, degree, pins,
+    grad_out, saved_agg, theta, tile_values, coords, live, degree, pins,
     out_cells, out_weight,
-    go, sa, th, tiles_own, tiles_far, inv_land, inv_far, inc, scaled,
+    go, sa, th, tiles_own, tiles_far, inv_vec, inv_land, inv_own, inv_far, inc, scaled, cells_sum,
     part, part_core, part_x, part_y, part_z, grads,
     wpart, wpart_core, wpart_x, wpart_y, wpart_z, wgrads,
     local_sem, send_sem, recv_sem,
@@ -141,8 +141,17 @@
         copies.append(copy)
         return copy
 
+    tile_copy = send(tile_values.at[0, 0], tiles_far.at[pl.ds(0, 16)], to_y)
+    place = lax.broadcasted_iota(jnp.int32, (8, 128), 1)
+    slots = jnp.full((8, 128), 16, jnp.int32)
+    for t in range(16):
+        code = coords[0, 0, 0, t] * 8 + coords[0, 0, 1, t]
+        code = jnp.where(t < live[0, 0], code, -1)
+        slots = jnp.where(place == code, t, slots)
+    inv_vec[...] = slots
     inv_copy = send(inv_vec, inv_land, to_y)
-    tile_copy = send(tile_values.at[0, 0], tiles_far.at[pl.ds(0, 16)], to_y)
+    own_move = pltpu.make_async_copy(inv_vec, inv_own, local_sem.at[5])
+    own_move.start()
 
     tile_len = tiles_own.shape[-1]
     zero_tile = jnp.zeros((tile_len, tile_len), BF16)
@@ -248,6 +257,7 @@
             scaled[h, :, i * n : (i + 1) * n] = (z_rows / root[:, i * n : (i + 1) * n]).astype(BF16)
 
     loads[2].wait()
+    own_move.wait()
     dense(tiles_own, inv_own, y)
     first = {}
     for side in (0, 1):
@@ -329,53 +339,87 @@
     for q, st in enumerate(main):
         st[5][core, mine + z] = (z_total(st, zs[q]) / pin_row).astype(BF16)
         zb.append(z_back(st))
+    row_block = 256
+
+    def cell_sum(h, pieces, start=False, last=False):
+        def rows(r, carry):
+            at = pl.ds(pl.multiple_of(r * row_block, row_block), row_block)
+            total = None if start else cells_sum[h, at, :]
+            for block, xt in pieces:
+                for p in range(2):
+                    j = block * 4 + xt * 2 + p
+                    net_rows = jnp.concatenate(
+                        [
+                            jnp.concatenate([grads[q, h, 2 * j], grads[q, h, 2 * j + 1]], axis=1)
+                            for q in range(CHUNKS)
+                        ],
+                        axis=0,
+                    )
+                    term = lax.dot_general(
+                        inc[j, at, :], net_rows, (((1,), (1,)), ((), ())), preferred_element_type=F32
+                    )
+                    total = term if total is None else total + term
+            if not last:
+                cells_sum[h, at, :] = total
+                return carry
+            for i in range(row_block // 128):
+                first_row = y * cells + r * row_block + i * 128
+                root_row = jnp.sqrt(
+                    degree[0:1, pl.ds(pl.multiple_of(first_row, 128), 128)].astype(F32)
+                )
+                root_tile = jnp.broadcast_to(root_row, (128, 128)).T
+                out_at = pl.ds(pl.multiple_of(r * row_block + i * 128, 128), 128)
+                for w in range(half // 128):
+                    out_cells[out_at, pl.ds(pl.multiple_of(h * half + w * 128, 128), 128)] = (
+                        total[i * 128 : (i + 1) * 128, w * 128 : (w + 1) * 128] / root_tile
+                    ).astype(BF16)
+            return carry
+
+        lax.fori_loop(0, cells // row_block, rows, 0)
+
+    yb, xb, cb = [], [], []
+    for q, st in enumerate(main):
+        for copy in zb[q]:
+            copy.wait_recv()
+        yb.append(forward(st, y, x, to_y))
+        xb.append(forward(st, y, x, to_x))
+        cb.append([forward(st, y, x, to_core)])
     w_yb.wait_recv()
     w_xb.append(forward(weight, 1 - y, x, to_x))
     w_cb.append(forward(weight, 1 - y, x, to_core))
-    yb, xb, cb = [], [], []
-    for q, st in enumerate(main):
-        for copy in zb[q]:
-            copy.wait_recv()
-        yb.append(forward(st, y, x, to_y))
-        xb.append([forward(st, y, x, to_x)])
-        cb.append(forward(st, y, x, to_core))
+    cell_sum(core, [(y, x)], start=True)
+    diagonal = []
+    for q, st in enumerate(main):
+        yb[q].wait_recv()
+        if q % 2 == 0:
+            diagonal.append(forward(st, 1 - y, x, to_x))
+        xb[q].wait_recv()
+        if q % 2 == 1:
+            diagonal.append(forward(st, y, 1 - x, to_y))
+        cb[q].append(forward(st, 1 - y, x, to_core))
+        cb[q].append(forward(st, y, 1 - x, to_core))
     for i in (0, 1):
         w_xb[i].wait_recv()
         w_cb.append(forward(weight, y if i == 0 else 1 - y, 1 - x, to_core))
-    for q, st in enumerate(main):
-        yb[q].wait_recv()
-        xb[q].append(forward(st, 1 - y, x, to_x))
-        cb.append(forward(st, 1 - y, x, to_core))
+    for q in range(CHUNKS):
+        cb[q][0].wait_recv()
+    cell_sum(1 - core, [(y, x)], start=True)
+    cell_sum(core, [(1 - y, x), (y, 1 - x)])
+    for q, st in enumerate(main):
+        diagonal[q].wait_recv()
+        cb[q].append(forward(st, 1 - y, 1 - x, to_core))
+    for q in range(CHUNKS):
+        cb[q][1].wait_recv()
+        cb[q][2].wait_recv()
+    cell_sum(1 - core, [(1 - y, x), (y, 1 - x)])
+    cell_sum(core, [(1 - y, 1 - x)], last=True)
     for copy in w_cb:
         copy.wait_recv()
     for t in range(32):
         out_weight[t * per : (t + 1) * per, :] = wgrads[t // 16, t % 16]
-    for i in (0, 1):
-        for q, st in enumerate(main):
-            xb[q][i].wait_recv()
-            cb.append(forward(st, y if i == 0 else 1 - y, 1 - x, to_core))
-    for copy in cb:
-        copy.wait_recv()
-
-    def cell_rows(r, carry):
-        at = pl.ds(pl.multiple_of(r * 128, 128), 128)
-        root_row = jnp.sqrt(
-            degree[0:1, pl.ds(pl.multiple_of(y * cells + r * 128, 128), 128)].astype(F32)
-        )
-        root_tile = jnp.broadcast_to(root_row, (128, 128)).T
-        for h in range(2):
-            for q in range(CHUNKS):
-                total = jnp.zeros((128, row_len), F32)
-                for j in range(8):
-                    net_rows = jnp.concatenate([grads[q, h, 2 * j], grads[q, h, 2 * j + 1]], axis=1)
-                    total = total + lax.dot_general(
-                        inc[j, at, :], net_rows, (((1,), (1,)), ((), ())), preferred_element_type=F32
-                    )
-                at_col = h * half + q * row_len
-                out_cells[at, at_col : at_col + row_len] = (total / root_tile[:, :row_len]).astype(BF16)
-        return carry
-
-    lax.fori_loop(0, cells // 128, cell_rows, 0)
+    for q in range(CHUNKS):
+        cb[q][3].wait_recv()
+    cell_sum(1 - core, [(1 - y, 1 - x)], last=True)
     for copy in copies:
         copy.wait_send()
 
@@ -387,13 +431,6 @@
     slots, tile_len = tile_values.shape[2], tile_values.shape[3]
     nets = net_pin_count.shape[0]
     net_tiles = nets // tile_len
-    places = jnp.arange(128, dtype=jnp.int32)
-    coords = tile_coords[0, 0]
-    slot = jnp.arange(slots, dtype=jnp.int32)
-    code = jnp.where(slot < block_tile_count[0, 0], coords[:, 0] * net_tiles + coords[:, 1], -1)
-    found = code[:, None] == places[None, :]
-    inv = slots + jnp.sum(jnp.where(found, slot[:, None] - slots, 0), axis=0)
-    inv = jnp.broadcast_to(inv[None, :], (8, 128)).astype(jnp.int32)
     half, row_len = width // 2, width // 2 // CHUNKS
     per = width // 32
     vmem = pltpu.VMEM
@@ -417,7 +454,7 @@
             jax.ShapeDtypeStruct((width, width), BF16),
         ),
         in_specs=[any_spec] * 4
-        + [vmem_spec, pl.BlockSpec(memory_space=pltpu.SMEM), vmem_spec, vmem_spec],
+        + [pl.BlockSpec(memory_space=pltpu.SMEM)] * 2 + [vmem_spec] * 2,
         out_specs=(vmem_spec, vmem_spec),
         scratch_shapes=[
             vmem((rows, width), BF16),
@@ -426,22 +463,25 @@
             vmem((slots + 1, tile_len, tile_len), BF16),
             vmem((slots + 1, tile_len, tile_len), BF16),
             vmem((8, 128), jnp.int32),
+            vmem((8, 128), jnp.int32),
+            pltpu.SMEM((8, 128), jnp.int32),
             pltpu.SMEM((8, 128), jnp.int32),
             vmem((net_tiles, rows, 2 * tile_len), BF16),
             vmem((2, half, rows), BF16),
+            vmem((2, rows, half), F32),
         ]
         + stage_buffers((CHUNKS,), (row_len, tile_len))
         + stage_buffers((), (per, width))
         + [
             pltpu.SemaphoreType.DMA((8,)),
-            pltpu.SemaphoreType.DMA((96,)),
-            pltpu.SemaphoreType.DMA((96,)),
+            pltpu.SemaphoreType.DMA((160,)),
+            pltpu.SemaphoreType.DMA((160,)),
         ],
         compiler_params=pltpu.CompilerParams(
-            collective_id=0, has_side_effects=True, vmem_limit_bytes=48 * 1024 * 1024
+            collective_id=0, has_side_effects=True, vmem_limit_bytes=60 * 1024 * 1024
         ),
     )(
-        grad_out, saved_agg, theta, tile_values, inv, inv,
+        grad_out, saved_agg, theta, tile_values, jnp.swapaxes(tile_coords, 2, 3), block_tile_count,
         cell_degree.reshape(1, -1), net_pin_count.reshape(1, -1),
     )
 

time: 73.2 us -> 64.2 us (0.88); the launches traced: 72 us -> 63.9 us
  local copies, waits for them, and re-layouts: 7.54 us -> 3.12 us
  Pallas kernels: 63 us -> 59.5 us
    unnamed x16 -> x4, local copies, waits for them, and re-layouts: 7.54 us -> 3.12 us
    pallas_call x1, Pallas kernels: 63 us -> 59.5 us  [fused_shards(): pl.pallas_call(exchange_kernel, out_shape=(jax.ShapeDtypeStruct((rows, wi...]
where the time goes in v2:
time: 64.2 us; the launch traced here: 63.9 us
  Pallas kernels  59.5 us (93%)
  local copies, waits for them, and re-layouts  3.12 us (5%)
  between operations  1.29 us (2%)
    pallas_call x1, Pallas kernels, fused_shards(): pl.pallas_call(exchange_kernel, out_shape=(jax.ShapeDtypeStruct((rows, wi...  59.5 us
    unnamed x4, local copies, waits for them, and re-layouts  3.12 us

profile of v2, /device:TPU:0, one launch (start us, length us, event | category | flops | bytes accessed | tf_op | source)
XLA Modules:
  0.0 63.9 jit_solution(17452208103095951357)
XLA Ops:
  1.3 59.5 %shard_map.95 = (bf16[1024,512]{1,0:T(8,128)(2,1)}, bf16[512,512]{1,0:T(8,128)(2,1)}) custom-call(bf16[1024,512]{1,0:T(8,128)(2,1)} %grad_out.1, bf16[1024,512]{1,0:T(8,128)(2,1)} %saved_agg.1, bf16[512,512]{1,0:T(8,128)(2,1)} %theta.1, bf16[1,1,16,128,128]{4,3,2,1,0:T(8,128)(2,1)} %tile_values.1, s32[1,1,2,16]{3,2,1,0:T(2,128)} %bitcast.5, ...), custom_call_target="tpu_custom_call" | custom-call | tf_op jit(solution)/shard_map/pallas_call | solution.py:450
  60.8 0.0 copy-start
  60.8 2.3 %copy.13 = bf16[1024,512]{1,0:T(8,128)(2,1)} copy(bf16[1024,512]{1,0:T(8,128)(2,1)} %get-tuple-element.4) | data formatting | bytes 2097152
  63.2 0.0 copy-done
  63.2 0.8 %copy.14 = bf16[512,512]{1,0:T(8,128)(2,1)} copy(bf16[512,512]{1,0:T(8,128)(2,1)S(1)} %copy-done) | data formatting | bytes 1048576
Async XLA Ops:
  60.8 2.3 %copy-start = (bf16[512,512]{1,0:T(8,128)(2,1)S(1)}, bf16[512,512]{1,0:T(8,128)(2,1)}, u32[]{:S(2)}) copy-start(bf16[512,512]{1,0:T(8,128)(2,1)} %get-tuple-element.5) | copy-start | bytes 1572868

commit v3 on v2

--- a/solution.py
+++ b/solution.py
@@ -97,8 +97,8 @@
     grad_out, saved_agg, theta, tile_values, coords, live, degree, pins,
     out_cells, out_weight,
     go, sa, th, tiles_own, tiles_far, inv_vec, inv_land, inv_own, inv_far, inc, scaled, cells_sum,
-    part, part_core, part_x, part_y, part_z, grads,
-    wpart, wpart_core, wpart_x, wpart_y, wpart_z, wgrads,
+    part, part_core, part_x, part_z, part_y, grads,
+    wpart, wpart_core, wpart_x, wpart_z, wpart_y, wgrads,
     local_sem, send_sem, recv_sem,
 ):
     cell = lax.axis_index("cells")
@@ -193,54 +193,55 @@
     def piece(block, xt):
         return pl.ds(block * 8 + xt * 4, 4)
 
-    main = [
-        (part.at[q], part_core.at[q], part_x.at[q], part_y.at[q], part_z.at[q], grads.at[q])
-        for q in range(CHUNKS)
-    ]
-    weight = (wpart, wpart_core, wpart_x, wpart_y, wpart_z, wgrads)
-
-    def core_send(st, block, xt):
-        return send(st[0].at[1 - core, piece(block, xt)], st[1].at[piece(block, xt)], to_core)
-
-    def core_add(st, copy, block, xt):
+    main = (part, part_core, part_x, part_z, part_y, grads)
+    weight = (wpart, wpart_core, wpart_x, wpart_z, wpart_y, wgrads)
+    whole, only = pl.ds(0, CHUNKS), pl.ds(0, 1)
+
+    def core_send(st, q, block, xt):
+        return send(st[0].at[q, 1 - core, piece(block, xt)], st[1].at[q, piece(block, xt)], to_core)
+
+    def core_add(st, q, copy, block, xt):
         copy.wait_recv()
         at = piece(block, xt)
-        st[0][core, at] = add(st[0][core, at], st[1][at])
-
-    def x_send(st, block):
-        return send(st[0].at[core, piece(block, 1 - x)], st[2].at[block], to_x)
-
-    def x_add(st, copy, block):
+        st[0][q, core, at] = add(st[0][q, core, at], st[1][q, at])
+
+    def x_send(st, q, block):
+        return send(st[0].at[q, core, piece(block, 1 - x)], st[2].at[q, block], to_x)
+
+    def x_add(st, q, copy, block):
         copy.wait_recv()
         at = piece(block, x)
-        st[0][core, at] = add(st[0][core, at], st[2][block])
-
-    def y_send(st):
-        return send(st[0].at[core, piece(1 - y, x)], st[3], to_y)
-
-    def y_add(st, copy):
-        copy.wait_recv()
-        at = piece(y, x)
-        st[0][core, at] = add(st[0][core, at], st[3][...])
-
-    mine = y * 8 + x * 4
-
-    def z_send(st):
-        return [send(st[0].at[core, mine + z_of[d]], st[4].at[d - 1], to_z[d]) for d in (1, 2, 3)]
-
-    def z_total(st, zs):
-        total = st[0][core, mine + z].astype(F32)
+        st[0][q, core, at] = add(st[0][q, core, at], st[2][q, block])
+
+    def tile_of(block, zt):
+        return block * 8 + x * 4 + zt
+
+    def z_send(st, q, block):
+        return [
+            send(st[0].at[q, core, tile_of(block, z_of[d])], st[3].at[q, block, d - 1], to_z[d])
+            for d in (1, 2, 3)
+        ]
+
+    def z_add(st, q, zs, block):
+        total = st[0][q, core, tile_of(block, z)].astype(F32)
         for d in (1, 2, 3):
             zs[d - 1].wait_recv()
-            total = total + st[4][d - 1].astype(F32)
-        return total
-
-    def z_back(st):
-        at = st[5].at[core, mine + z]
+            total = total + st[3][q, block, d - 1].astype(F32)
+        st[0][q, core, tile_of(block, z)] = total.astype(BF16)
+
+    def y_send(st, q):
+        return send(st[0].at[q, core, tile_of(1 - y, z)], st[4].at[q], to_y)
+
+    def y_total(st, q, copy):
+        copy.wait_recv()
+        return st[0][q, core, tile_of(y, z)].astype(F32) + st[4][q].astype(F32)
+
+    def z_back(st, q):
+        at = st[5].at[q, core, tile_of(y, z)]
         return [send(at, at, to_z[d]) for d in (1, 2, 3)]
 
-    def forward(st, block, xt, target):
-        at = st[5].at[core, piece(block, xt)]
+    def forward(st, q, block, xt, target):
+        at = st[5].at[q, core, piece(block, xt)]
         return send(at, at, target)
 
     loads[0].wait()
@@ -259,86 +260,60 @@
     loads[2].wait()
     own_move.wait()
     dense(tiles_own, inv_own, y)
-    first = {}
+    own = {}
     for side in (0, 1):
         xt = 1 - x if side == 0 else x
         net_part(1 - core, y, xt)
-        first[side] = [core_send(st, y, xt) for st in main]
+        own[side] = core_send(main, whole, y, xt)
         net_part(core, y, xt)
-    x_own = []
-    for q, st in enumerate(main):
-        core_add(st, first[0][q], y, 1 - x)
-        x_own.append(x_send(st, y))
+    core_add(main, whole, own[0], y, 1 - x)
+    own_x = x_send(main, whole, y)
 
     loads[3].wait()
-    per = wpart.shape[2]
+    per = wpart.shape[3]
 
     def weight_rows(i, carry):
         rows = sa[:, pl.ds(pl.multiple_of(i * 128, 128), 128)]
         term = lax.dot_general(rows, go[...], (((0,), (0,)), ((), ())), preferred_element_type=F32)
         term = term.astype(BF16)
         for j in range(128 // per):
-            wpart[i // 2, (i % 2) * (128 // per) + j] = term[j * per : (j + 1) * per]
+            wpart[0, i // 2, (i % 2) * (128 // per) + j] = term[j * per : (j + 1) * per]
         return carry
 
     lax.fori_loop(0, 4, weight_rows, 0)
     w_core = {}
-    for block in (0, 1):
-        for side in (0, 1):
-            w_core[block, side] = core_send(weight, block, 1 - x if side == 0 else x)
-    for q, st in enumerate(main):
-        core_add(st, first[1][q], y, x)
+    for side in (0, 1):
+        for block in (0, 1):
+            w_core[block, side] = core_send(weight, only, block, 1 - x if side == 0 else x)
+    core_add(main, whole, own[1], y, x)
     w_x = []
     for block in (0, 1):
-        core_add(weight, w_core[block, 0], block, 1 - x)
-        w_x.append(x_send(weight, block))
+        core_add(weight, only, w_core[block, 0], block, 1 - x)
+        w_x.append(x_send(weight, only, block))
     for block in (0, 1):
-        core_add(weight, w_core[block, 1], block, x)
-    for q, st in enumerate(main):
-        x_add(st, x_own[q], y)
-    for block in (0, 1):
-        x_add(weight, w_x[block], block)
+        core_add(weight, only, w_core[block, 1], block, x)
+    x_add(main, whole, own_x, y)
+    own_z = z_send(main, whole, y)
 
     inv_copy.wait_recv()
     inv_move = pltpu.make_async_copy(inv_land, inv_far, local_sem.at[4])
     inv_move.start()
     inv_move.wait()
     tile_copy.wait_recv()
-    w_y = y_send(weight)
     dense(tiles_far, inv_far, 1 - y)
+    far = {}
+    chunk = [pl.ds(q, 1) for q in range(CHUNKS)]
     for side in (0, 1):
         xt = 1 - x if side == 0 else x
         net_part(1 - core, 1 - y, xt)
-        first[side] = [core_send(st, 1 - y, xt) for st in main]
+        far[side] = [core_send(main, q, 1 - y, xt) for q in chunk]
         net_part(core, 1 - y, xt)
-    x_far = []
-    for q, st in enumerate(main):
-        core_add(st, first[0][q], 1 - y, 1 - x)
-        x_far.append(x_send(st, 1 - y))
-    for q, st in enumerate(main):
-        core_add(st, first[1][q], 1 - y, x)
-    y_add(weight, w_y)
-    w_z = z_send(weight)
-    ys = []
-    for q, st in enumerate(main):
-        x_add(st, x_far[q], 1 - y)
-        ys.append(y_send(st))
-    weight[5][core, mine + z] = z_total(weight, w_z).astype(BF16)
-    w_zb = z_back(weight)
-    zs = []
-    for q, st in enumerate(main):
-        y_add(st, ys[q])
-        zs.append(z_send(st))
-    for copy in w_zb:
-        copy.wait_recv()
-    w_yb = forward(weight, y, x, to_y)
-    w_xb = [forward(weight, y, x, to_x)]
-    w_cb = [forward(weight, y, x, to_core)]
+    w_z = []
+    for block in (0, 1):
+        x_add(weight, only, w_x[block], block)
+        w_z.append(z_send(weight, only, block))
+
     pin_row = pins[0:1, pl.ds(pl.multiple_of((x * 4 + z) * tile_len, tile_len), tile_len)].astype(F32)
-    zb = []
-    for q, st in enumerate(main):
-        st[5][core, mine + z] = (z_total(st, zs[q]) / pin_row).astype(BF16)
-        zb.append(z_back(st))
     row_block = 256
 
     def cell_sum(h, pieces, start=False, last=False):
@@ -377,48 +352,119 @@
 
         lax.fori_loop(0, cells // row_block, rows, 0)
 
-    yb, xb, cb = [], [], []
-    for q, st in enumerate(main):
-        for copy in zb[q]:
-            copy.wait_recv()
-        yb.append(forward(st, y, x, to_y))
-        xb.append(forward(st, y, x, to_x))
-        cb.append([forward(st, y, x, to_core)])
-    w_yb.wait_recv()
-    w_xb.append(forward(weight, 1 - y, x, to_x))
-    w_cb.append(forward(weight, 1 - y, x, to_core))
-    cell_sum(core, [(y, x)], start=True)
-    diagonal = []
-    for q, st in enumerate(main):
-        yb[q].wait_recv()
-        if q % 2 == 0:
-            diagonal.append(forward(st, 1 - y, x, to_x))
-        xb[q].wait_recv()
-        if q % 2 == 1:
-            diagonal.append(forward(st, y, 1 - x, to_y))
-        cb[q].append(forward(st, 1 - y, x, to_core))
-        cb[q].append(forward(st, y, 1 - x, to_core))
-    for i in (0, 1):
-        w_xb[i].wait_recv()
-        w_cb.append(forward(weight, y if i == 0 else 1 - y, 1 - x, to_core))
+    steps = []
+
+    def step(when):
+        def put(run):
+            steps.append((when, len(steps), run))
+            return run
+
+        return put
+
+    def gather_steps(st, q, start, gap, z_copies):
+        got = {}
+
+        @step(start)
+        def _():
+            for copy in z_copies():
+                copy.wait_recv()
+            got["x"] = forward(st, q, y, x, to_x)
+            got["y"] = forward(st, q, y, x, to_y)
+            got["core"] = [forward(st, q, y, x, to_core)]
+
+        @step(start + gap)
+        def _():
+            got["x"].wait_recv()
+            got["diagonal"] = forward(st, q, y, 1 - x, to_y)
+            got["core"].append(forward(st, q, y, 1 - x, to_core))
+            got["y"].wait_recv()
+            got["core"].append(forward(st, q, 1 - y, x, to_core))
+
+        @step(start + 2 * gap)
+        def _():
+            got["diagonal"].wait_recv()
+            got["core"].append(forward(st, q, 1 - y, 1 - x, to_core))
+
+        return got
+
+    def chunk_steps(q, start, gap):
+        state = {}
+
+        @step(0)
+        def _():
+            core_add(main, chunk[q], far[0][q], 1 - y, 1 - x)
+            state["x"] = x_send(main, chunk[q], 1 - y)
+
+        @step(start + 0.5 * gap)
+        def _():
+            core_add(main, chunk[q], far[1][q], 1 - y, x)
+
+        @step(start + gap)
+        def _():
+            x_add(main, chunk[q], state["x"], 1 - y)
+            state["z"] = z_send(main, chunk[q], 1 - y)
+
+        @step(start + 2 * gap)
+        def _():
+            z_add(main, chunk[q], state["z"], 1 - y)
+            state["y"] = y_send(main, chunk[q])
+
+        @step(start + 3 * gap)
+        def _():
+            total = y_total(main, chunk[q], state["y"])
+            grads[chunk[q], core, tile_of(y, z)] = (total / pin_row).astype(BF16)
+            state["back"] = z_back(main, chunk[q])
+
+        return gather_steps(main, chunk[q], start + 4 * gap, gap, lambda: state["back"])
+
+    gap = 2.0
+    got = [chunk_steps(q, q * 1.0, gap) for q in range(CHUNKS)]
+    w_state = {}
+
+    @step(0.5 * gap + 0.1)
+    def _():
+        for block in (0, 1):
+            z_add(weight, only, w_z[block], block)
+        w_state["y"] = y_send(weight, only)
+
+    @step(1.5 * gap)
+    def _():
+        z_add(main, whole, own_z, y)
+
+    @step(2 * gap - 0.1)
+    def _():
+        total = y_total(weight, only, w_state["y"])
+        wgrads[only, core, tile_of(y, z)] = total.astype(BF16)
+        w_state["back"] = z_back(weight, only)
+
+    w_got = gather_steps(weight, only, 3 * gap + 0.1, 1.5 * gap, lambda: w_state["back"])
+    late = 4 * gap + CHUNKS - 1
+
+    @step(late + 0.1)
+    def _():
+        cell_sum(core, [(y, x)], start=True)
+
+    @step(late + gap + 0.1)
+    def _():
+        for q in range(CHUNKS):
+            got[q]["core"][0].wait_recv()
+        cell_sum(1 - core, [(y, x)], start=True)
+        cell_sum(core, [(1 - y, x), (y, 1 - x)])
+
+    for _, _, run in sorted(steps, key=lambda entry: entry[:2]):
+        run()
+
     for q in range(CHUNKS):
-        cb[q][0].wait_recv()
-    cell_sum(1 - core, [(y, x)], start=True)
-    cell_sum(core, [(1 - y, x), (y, 1 - x)])
-    for q, st in enumerate(main):
-        diagonal[q].wait_recv()
-        cb[q].append(forward(st, 1 - y, 1 - x, to_core))
-    for q in range(CHUNKS):
-        cb[q][1].wait_recv()
-        cb[q][2].wait_recv()
+        got[q]["core"][1].wait_recv()
+        got[q]["core"][2].wait_recv()
     cell_sum(1 - core, [(1 - y, x), (y, 1 - x)])
     cell_sum(core, [(1 - y, 1 - x)], last=True)
-    for copy in w_cb:
+    for copy in w_got["core"]:
         copy.wait_recv()
     for t in range(32):
-        out_weight[t * per : (t + 1) * per, :] = wgrads[t // 16, t % 16]
+        out_weight[t * per : (t + 1) * per, :] = wgrads[0, t // 16, t % 16]
     for q in range(CHUNKS):
-        cb[q][3].wait_recv()
+        got[q]["core"][3].wait_recv()
     cell_sum(1 - core, [(1 - y, 1 - x)], last=True)
     for copy in copies:
         copy.wait_send()
@@ -442,8 +488,8 @@
             vmem(lead + (2, 16) + block, BF16),
             vmem(lead + (16,) + block, BF16),
             vmem(lead + (2, 4) + block, BF16),
-            vmem(lead + (4,) + block, BF16),
-            vmem(lead + (3,) + block, BF16),
+            vmem(lead + (2, 3) + block, BF16),
+            vmem(lead + block, BF16),
             vmem(lead + (2, 16) + block, BF16),
         ]
 
@@ -471,7 +517,7 @@
             vmem((2, rows, half), F32),
         ]
         + stage_buffers((CHUNKS,), (row_len, tile_len))
-        + stage_buffers((), (per, width))
+        + stage_buffers((1,), (per, width))
         + [
             pltpu.SemaphoreType.DMA((8,)),
             pltpu.SemaphoreType.DMA((160,)),

time: 64.2 us -> 65.1 us (1.014)
  Pallas kernels: 59.5 us -> 60.5 us
    pallas_call x1, Pallas kernels: 59.5 us -> 60.5 us  [fused_shards(): pl.pallas_call(exchange_kernel, out_shape=(jax.ShapeDtypeStruct((rows, wi...]
where the time goes in v3:
time: 65.1 us; the launch traced here: 64.9 us
  Pallas kernels  60.5 us (93%)
  local copies, waits for them, and re-layouts  3.12 us (5%)
  between operations  1.29 us (2%)
    pallas_call x1, Pallas kernels, fused_shards(): pl.pallas_call(exchange_kernel, out_shape=(jax.ShapeDtypeStruct((rows, wi...  60.5 us
    unnamed x4, local copies, waits for them, and re-layouts  3.12 us

profile of v3, /device:TPU:0, one launch (start us, length us, event | category | flops | bytes accessed | tf_op | source)
XLA Modules:
  0.0 64.9 jit_solution(17361809332512991788)
XLA Ops:
  1.3 60.5 %shard_map.95 = (bf16[1024,512]{1,0:T(8,128)(2,1)}, bf16[512,512]{1,0:T(8,128)(2,1)}) custom-call(bf16[1024,512]{1,0:T(8,128)(2,1)} %grad_out.1, bf16[1024,512]{1,0:T(8,128)(2,1)} %saved_agg.1, bf16[512,512]{1,0:T(8,128)(2,1)} %theta.1, bf16[1,1,16,128,128]{4,3,2,1,0:T(8,128)(2,1)} %tile_values.1, s32[1,1,2,16]{3,2,1,0:T(2,128)} %bitcast.5, ...), custom_call_target="tpu_custom_call" | custom-call | tf_op jit(solution)/shard_map/pallas_call | solution.py:496
  61.7 0.0 copy-start
  61.8 2.3 %copy.13 = bf16[1024,512]{1,0:T(8,128)(2,1)} copy(bf16[1024,512]{1,0:T(8,128)(2,1)} %get-tuple-element.4) | data formatting | bytes 2097152
  64.1 0.0 copy-done
  64.1 0.8 %copy.14 = bf16[512,512]{1,0:T(8,128)(2,1)} copy(bf16[512,512]{1,0:T(8,128)(2,1)S(1)} %copy-done) | data formatting | bytes 1048576
Async XLA Ops:
  61.7 2.3 %copy-start = (bf16[512,512]{1,0:T(8,128)(2,1)S(1)}, bf16[512,512]{1,0:T(8,128)(2,1)}, u32[]{:S(2)}) copy-start(bf16[512,512]{1,0:T(8,128)(2,1)} %get-tuple-element.5) | copy-start | bytes 1572868

commit v4 on v3

--- a/solution.py
+++ b/solution.py
@@ -99,7 +99,7 @@
     go, sa, th, tiles_own, tiles_far, inv_vec, inv_land, inv_own, inv_far, inc, scaled, cells_sum,
     part, part_core, part_x, part_z, part_y, grads,
     wpart, wpart_core, wpart_x, wpart_z, wpart_y, wgrads,
-    local_sem, send_sem, recv_sem,
+    local_sem, send_sem, recv_sem, pair_send, pair_recv,
 ):
     cell = lax.axis_index("cells")
     y = lax.axis_index("nets")
@@ -171,21 +171,34 @@
 
         lax.fori_loop(0, 8, row, 0)
 
-    half = scaled.shape[1]
+    half = scaled.shape[0] // 2
     row_len = part.shape[3]
 
-    def net_part(h, block, xt):
-        def pair(p, carry):
-            j = block * 4 + xt * 2 + p
-            product = jnp.dot(scaled[h], inc[j], preferred_element_type=F32).astype(BF16)
-            for q in range(CHUNKS):
-                for s in range(2):
-                    part[q, h, j * 2 + s] = product[
-                        q * row_len : (q + 1) * row_len, s * tile_len : (s + 1) * tile_len
-                    ]
+    def core_copy(block, p):
+        pair = block * 4 + lax.rem((1 - x) * 2 + p, 4)
+        i = (block + y) % 2 * 4 + p
+        at = pl.ds(pair * 2, 2)
+        return pltpu.make_async_remote_copy(
+            src_ref=part.at[:, 1 - core, at], dst_ref=part_core.at[:, at],
+            send_sem=pair_send.at[i], recv_sem=pair_recv.at[i],
+            device_id=to_core, device_id_type=MESH,
+        )
+
+    def net_part(block):
+        def step(p, carry):
+            j = block * 4 + lax.rem((1 - x) * 2 + p, 4)
+            product = jnp.dot(scaled[...], inc[j], preferred_element_type=F32).astype(BF16)
+            for h in range(2):
+                for q in range(CHUNKS):
+                    row = h * half + q * row_len
+                    for s in range(2):
+                        part[q, h, j * 2 + s] = product[
+                            row : row + row_len, s * tile_len : (s + 1) * tile_len
+                        ]
+            core_copy(block, p).start()
             return carry
 
-        lax.fori_loop(0, 2, pair, 0)
+        lax.fori_loop(0, 4, step, 0)
 
     def add(a, b):
         return (a.astype(F32) + b.astype(F32)).astype(BF16)
@@ -201,7 +214,8 @@
         return send(st[0].at[q, 1 - core, piece(block, xt)], st[1].at[q, piece(block, xt)], to_core)
 
     def core_add(st, q, copy, block, xt):
-        copy.wait_recv()
+        if copy is not None:
+            copy.wait_recv()
         at = piece(block, xt)
         st[0][q, core, at] = add(st[0][q, core, at], st[1][q, at])
 
@@ -247,26 +261,25 @@
     loads[0].wait()
     loads[1].wait()
     cells = go.shape[0]
-    root = jnp.sqrt(degree[0:1, pl.ds(pl.multiple_of(y * cells, cells), cells)].astype(F32))
-    for i in range(4):
-        n = cells // 4
-        for h in range(2):
-            z_rows = lax.dot_general(
-                th[h * half : (h + 1) * half], go[i * n : (i + 1) * n], (((1,), (1,)), ((), ())),
-                preferred_element_type=F32,
-            )
-            scaled[h, :, i * n : (i + 1) * n] = (z_rows / root[:, i * n : (i + 1) * n]).astype(BF16)
-
+
+    def scale_rows(i, carry):
+        at = pl.ds(pl.multiple_of(i * 256, 256), 256)
+        z_rows = lax.dot_general(
+            th[...], go[at, :], (((1,), (1,)), ((), ())), preferred_element_type=F32
+        )
+        at_degree = pl.ds(pl.multiple_of(y * cells + i * 256, 256), 256)
+        root = jnp.sqrt(degree[0:1, at_degree].astype(F32))
+        scaled[:, at] = (z_rows / root).astype(BF16)
+        return carry
+
+    lax.fori_loop(0, cells // 256, scale_rows, 0)
     loads[2].wait()
     own_move.wait()
     dense(tiles_own, inv_own, y)
-    own = {}
-    for side in (0, 1):
-        xt = 1 - x if side == 0 else x
-        net_part(1 - core, y, xt)
-        own[side] = core_send(main, whole, y, xt)
-        net_part(core, y, xt)
-    core_add(main, whole, own[0], y, 1 - x)
+    net_part(y)
+    for p in (0, 1):
+        core_copy(y, p).wait_recv()
+    core_add(main, whole, None, y, 1 - x)
     own_x = x_send(main, whole, y)
 
     loads[3].wait()
@@ -285,7 +298,9 @@
     for side in (0, 1):
         for block in (0, 1):
             w_core[block, side] = core_send(weight, only, block, 1 - x if side == 0 else x)
-    core_add(main, whole, own[1], y, x)
+    for p in (2, 3):
+        core_copy(y, p).wait_recv()
+    core_add(main, whole, None, y, x)
     w_x = []
     for block in (0, 1):
         core_add(weight, only, w_core[block, 0], block, 1 - x)
@@ -301,13 +316,8 @@
     inv_move.wait()
     tile_copy.wait_recv()
     dense(tiles_far, inv_far, 1 - y)
-    far = {}
     chunk = [pl.ds(q, 1) for q in range(CHUNKS)]
-    for side in (0, 1):
-        xt = 1 - x if side == 0 else x
-        net_part(1 - core, 1 - y, xt)
-        far[side] = [core_send(main, q, 1 - y, xt) for q in chunk]
-        net_part(core, 1 - y, xt)
+    net_part(1 - y)
     w_z = []
     for block in (0, 1):
         x_add(weight, only, w_x[block], block)
@@ -316,41 +326,46 @@
     pin_row = pins[0:1, pl.ds(pl.multiple_of((x * 4 + z) * tile_len, tile_len), tile_len)].astype(F32)
     row_block = 256
 
-    def cell_sum(h, pieces, start=False, last=False):
+    def cell_sum(h, pieces, start=False):
         def rows(r, carry):
-            at = pl.ds(pl.multiple_of(r * row_block, row_block), row_block)
+            at = pl.ds(pl.multiple_of(lax.rem(r, 4) * row_block, row_block), row_block)
+            block, xt = pieces(r // 4)
             total = None if start else cells_sum[h, at, :]
-            for block, xt in pieces:
-                for p in range(2):
-                    j = block * 4 + xt * 2 + p
-                    net_rows = jnp.concatenate(
-                        [
-                            jnp.concatenate([grads[q, h, 2 * j], grads[q, h, 2 * j + 1]], axis=1)
-                            for q in range(CHUNKS)
-                        ],
-                        axis=0,
-                    )
-                    term = lax.dot_general(
-                        inc[j, at, :], net_rows, (((1,), (1,)), ((), ())), preferred_element_type=F32
-                    )
-                    total = term if total is None else total + term
-            if not last:
-                cells_sum[h, at, :] = total
-                return carry
-            for i in range(row_block // 128):
-                first_row = y * cells + r * row_block + i * 128
-                root_row = jnp.sqrt(
-                    degree[0:1, pl.ds(pl.multiple_of(first_row, 128), 128)].astype(F32)
+            for p in range(2):
+                j = block * 4 + xt * 2 + p
+                net_rows = jnp.concatenate(
+                    [
+                        jnp.concatenate([grads[q, h, 2 * j], grads[q, h, 2 * j + 1]], axis=1)
+                        for q in range(CHUNKS)
+                    ],
+                    axis=0,
                 )
-                root_tile = jnp.broadcast_to(root_row, (128, 128)).T
-                out_at = pl.ds(pl.multiple_of(r * row_block + i * 128, 128), 128)
-                for w in range(half // 128):
-                    out_cells[out_at, pl.ds(pl.multiple_of(h * half + w * 128, 128), 128)] = (
-                        total[i * 128 : (i + 1) * 128, w * 128 : (w + 1) * 128] / root_tile
-                    ).astype(BF16)
+                term = lax.dot_general(
+                    inc[j, at, :], net_rows, (((1,), (1,)), ((), ())), preferred_element_type=F32
+                )
+                total = term if total is None else total + term
+            cells_sum[h, at, :] = total
             return carry
 
-        lax.fori_loop(0, cells // row_block, rows, 0)
+        return rows
+
+    def run_sum(h, pieces, count, start=False):
+        lax.fori_loop(0, count * (cells // row_block), cell_sum(h, pieces, start), 0)
+
+    def sides(i):
+        return lax.rem(1 - y + i, 2), lax.rem(x + i, 2)
+
+    def store_rows(i, carry):
+        at = pl.ds(pl.multiple_of(i * 128, 128), 128)
+        at_degree = pl.ds(pl.multiple_of(y * cells + i * 128, 128), 128)
+        root_row = jnp.sqrt(degree[0:1, at_degree].astype(F32))
+        root_tile = jnp.broadcast_to(root_row, (128, 128)).T
+        for h in range(2):
+            for w in range(half // 128):
+                out_cells[at, h * half + w * 128 : h * half + (w + 1) * 128] = (
+                    cells_sum[h, at, w * 128 : (w + 1) * 128] / root_tile
+                ).astype(BF16)
+        return carry
 
     steps = []
 
@@ -392,12 +407,18 @@
 
         @step(0)
         def _():
-            core_add(main, chunk[q], far[0][q], 1 - y, 1 - x)
+            if q == 0:
+                for p in (0, 1):
+                    core_copy(1 - y, p).wait_recv()
+            core_add(main, chunk[q], None, 1 - y, 1 - x)
             state["x"] = x_send(main, chunk[q], 1 - y)
 
         @step(start + 0.5 * gap)
         def _():
-            core_add(main, chunk[q], far[1][q], 1 - y, x)
+            if q == 0:
+                for p in (2, 3):
+                    core_copy(1 - y, p).wait_recv()
+            core_add(main, chunk[q], None, 1 - y, x)
 
         @step(start + gap)
         def _():
@@ -442,14 +463,14 @@
 
     @step(late + 0.1)
     def _():
-        cell_sum(core, [(y, x)], start=True)
+        run_sum(core, lambda i: (y, x), 1, start=True)
 
     @step(late + gap + 0.1)
     def _():
         for q in range(CHUNKS):
             got[q]["core"][0].wait_recv()
-        cell_sum(1 - core, [(y, x)], start=True)
-        cell_sum(core, [(1 - y, x), (y, 1 - x)])
+        run_sum(1 - core, lambda i: (y, x), 1, start=True)
+        run_sum(core, sides, 2)
 
     for _, _, run in sorted(steps, key=lambda entry: entry[:2]):
         run()
@@ -457,15 +478,23 @@
     for q in range(CHUNKS):
         got[q]["core"][1].wait_recv()
         got[q]["core"][2].wait_recv()
-    cell_sum(1 - core, [(1 - y, x), (y, 1 - x)])
-    cell_sum(core, [(1 - y, 1 - x)], last=True)
+    run_sum(1 - core, sides, 2)
+    run_sum(core, lambda i: (1 - y, 1 - x), 1)
     for copy in w_got["core"]:
         copy.wait_recv()
-    for t in range(32):
-        out_weight[t * per : (t + 1) * per, :] = wgrads[0, t // 16, t % 16]
+
+    def store_weight(t, carry):
+        out_weight[pl.ds(pl.multiple_of(t * per, per), per), :] = wgrads[0, t // 16, lax.rem(t, 16)]
+        return carry
+
+    lax.fori_loop(0, 32, store_weight, 0)
     for q in range(CHUNKS):
         got[q]["core"][3].wait_recv()
-    cell_sum(1 - core, [(1 - y, 1 - x)], last=True)
+    run_sum(1 - core, lambda i: (1 - y, 1 - x), 1)
+    lax.fori_loop(0, cells // 128, store_rows, 0)
+    for block in (y, 1 - y):
+        for p in range(4):
+            core_copy(block, p).wait_send()
     for copy in copies:
         copy.wait_send()
 
@@ -496,8 +525,8 @@
     return pl.pallas_call(
         exchange_kernel,
         out_shape=(
-            jax.ShapeDtypeStruct((rows, width), BF16),
-            jax.ShapeDtypeStruct((width, width), BF16),
+            pltpu.VMEM((rows, width), BF16),
+            pltpu.VMEM((width, width), BF16),
         ),
         in_specs=[any_spec] * 4
         + [pl.BlockSpec(memory_space=pltpu.SMEM)] * 2 + [vmem_spec] * 2,
@@ -513,7 +542,7 @@
             pltpu.SMEM((8, 128), jnp.int32),
             pltpu.SMEM((8, 128), jnp.int32),
             vmem((net_tiles, rows, 2 * tile_len), BF16),
-            vmem((2, half, rows), BF16),
+            vmem((width, rows), BF16),
             vmem((2, rows, half), F32),
         ]
         + stage_buffers((CHUNKS,), (row_len, tile_len))
@@ -522,6 +551,8 @@
             pltpu.SemaphoreType.DMA((8,)),
             pltpu.SemaphoreType.DMA((160,)),
             pltpu.SemaphoreType.DMA((160,)),
+            pltpu.SemaphoreType.DMA((8,)),
+            pltpu.SemaphoreType.DMA((8,)),
         ],
         compiler_params=pltpu.CompilerParams(
             collective_id=0, has_side_effects=True, vmem_limit_bytes=60 * 1024 * 1024

time: 65.1 us -> 66.7 us (1.025)
  Pallas kernels: 60.5 us -> 63.4 us
  local copies, waits for them, and re-layouts: 3.12 us -> 1.77 us
    pallas_call x1, Pallas kernels: 60.5 us -> 63.4 us  [fused_shards(): pl.pallas_call(exchange_kernel, out_shape=(pltpu.VMEM((rows, width), BF16...]
    unnamed x4 -> x2, local copies, waits for them, and re-layouts: 3.12 us -> 1.77 us
where the time goes in v4:
time: 66.7 us; the launch traced here: 66.5 us
  Pallas kernels  63.4 us (95%)
  local copies, waits for them, and re-layouts  1.77 us (3%)
  between operations  1.29 us (2%)
    pallas_call x1, Pallas kernels, fused_shards(): pl.pallas_call(exchange_kernel, out_shape=(pltpu.VMEM((rows, width), BF16...  63.4 us
    unnamed x2, local copies, waits for them, and re-layouts  1.77 us

profile of v4, /device:TPU:0, one launch (start us, length us, event | category | flops | bytes accessed | tf_op | source)
XLA Modules:
  0.0 66.5 jit_solution(3360868516944476159)
XLA Ops:
  1.3 63.4 %shard_map.95 = (bf16[1024,512]{1,0:T(8,128)(2,1)S(1)}, bf16[512,512]{1,0:T(8,128)(2,1)S(1)}) custom-call(bf16[1024,512]{1,0:T(8,128)(2,1)} %grad_out.1, bf16[1024,512]{1,0:T(8,128)(2,1)} %saved_agg.1, bf16[512,512]{1,0:T(8,128)(2,1)} %theta.1, bf16[1,1,16,128,128]{4,3,2,1,0:T(8,128)(2,1)} %tile_values.1, s32[1,1,2,16]{3,2,1,0:T(2,128)} %bitcast.5, ...), custom_call_target="tpu_custom_call" | custom-call | tf_op jit(solution)/shard_map/pallas_call | solution.py:525
  64.7 1.0 %copy.12 = bf16[1024,512]{1,0:T(8,128)(2,1)} copy(bf16[1024,512]{1,0:T(8,128)(2,1)S(1)} %get-tuple-element.2) | data formatting | bytes 2097152
  65.7 0.8 %copy.13 = bf16[512,512]{1,0:T(8,128)(2,1)} copy(bf16[512,512]{1,0:T(8,128)(2,1)S(1)} %get-tuple-element.3) | data formatting | bytes 1048576

commit v5 on v3

--- a/solution.py
+++ b/solution.py
@@ -8,7 +8,7 @@
 from jax.sharding import PartitionSpec as P
 
 TBLK = 16
-CHUNKS = 4
+CHUNKS = 2
 F32 = jnp.float32
 BF16 = jnp.bfloat16
 MESH = pl.DeviceIdType.MESH
@@ -496,8 +496,8 @@
     return pl.pallas_call(
         exchange_kernel,
         out_shape=(
-            jax.ShapeDtypeStruct((rows, width), BF16),
-            jax.ShapeDtypeStruct((width, width), BF16),
+            pltpu.VMEM((rows, width), BF16),
+            pltpu.VMEM((width, width), BF16),
         ),
         in_specs=[any_spec] * 4
         + [pl.BlockSpec(memory_space=pltpu.SMEM)] * 2 + [vmem_spec] * 2,

time: 65.1 us -> 62.1 us (0.954)
  Pallas kernels: 60.5 us -> 58.8 us
  local copies, waits for them, and re-layouts: 3.12 us -> 1.77 us
    pallas_call x1, Pallas kernels: 60.5 us -> 58.8 us  [fused_shards(): pl.pallas_call(exchange_kernel, out_shape=(pltpu.VMEM((rows, width), BF16...]
    unnamed x4 -> x2, local copies, waits for them, and re-layouts: 3.12 us -> 1.77 us
where the time goes in v5:
time: 62.1 us; the launch traced here: 61.9 us
  Pallas kernels  58.8 us (95%)
  local copies, waits for them, and re-layouts  1.77 us (3%)
  between operations  1.29 us (2%)
    pallas_call x1, Pallas kernels, fused_shards(): pl.pallas_call(exchange_kernel, out_shape=(pltpu.VMEM((rows, width), BF16...  58.8 us
    unnamed x2, local copies, waits for them, and re-layouts  1.77 us

profile of v5, /device:TPU:0, one launch (start us, length us, event | category | flops | bytes accessed | tf_op | source)
XLA Modules:
  0.0 61.9 jit_solution(4700597635964598858)
XLA Ops:
  1.3 58.8 %shard_map.95 = (bf16[1024,512]{1,0:T(8,128)(2,1)S(1)}, bf16[512,512]{1,0:T(8,128)(2,1)S(1)}) custom-call(bf16[1024,512]{1,0:T(8,128)(2,1)} %grad_out.1, bf16[1024,512]{1,0:T(8,128)(2,1)} %saved_agg.1, bf16[512,512]{1,0:T(8,128)(2,1)} %theta.1, bf16[1,1,16,128,128]{4,3,2,1,0:T(8,128)(2,1)} %tile_values.1, s32[1,1,2,16]{3,2,1,0:T(2,128)} %bitcast.5, ...), custom_call_target="tpu_custom_call" | custom-call | tf_op jit(solution)/shard_map/pallas_call | solution.py:496
  60.1 1.0 %copy.12 = bf16[1024,512]{1,0:T(8,128)(2,1)} copy(bf16[1024,512]{1,0:T(8,128)(2,1)S(1)} %get-tuple-element.2) | data formatting | bytes 2097152
  61.1 0.8 %copy.13 = bf16[512,512]{1,0:T(8,128)(2,1)} copy(bf16[512,512]{1,0:T(8,128)(2,1)S(1)} %get-tuple-element.3) | data formatting | bytes 1048576

commit v6 on v5

--- a/solution.py
+++ b/solution.py
@@ -265,9 +265,10 @@
         xt = 1 - x if side == 0 else x
         net_part(1 - core, y, xt)
         own[side] = core_send(main, whole, y, xt)
+        if side == 1:
+            core_add(main, whole, own[0], y, 1 - x)
+            own_x = x_send(main, whole, y)
         net_part(core, y, xt)
-    core_add(main, whole, own[0], y, 1 - x)
-    own_x = x_send(main, whole, y)
 
     loads[3].wait()
     per = wpart.shape[3]
@@ -292,8 +293,6 @@
         w_x.append(x_send(weight, only, block))
     for block in (0, 1):
         core_add(weight, only, w_core[block, 1], block, x)
-    x_add(main, whole, own_x, y)
-    own_z = z_send(main, whole, y)
 
     inv_copy.wait_recv()
     inv_move = pltpu.make_async_copy(inv_land, inv_far, local_sem.at[4])
@@ -301,13 +300,19 @@
     inv_move.wait()
     tile_copy.wait_recv()
     dense(tiles_far, inv_far, 1 - y)
-    far = {}
+    far, far_x = {}, []
     chunk = [pl.ds(q, 1) for q in range(CHUNKS)]
     for side in (0, 1):
         xt = 1 - x if side == 0 else x
         net_part(1 - core, 1 - y, xt)
         far[side] = [core_send(main, q, 1 - y, xt) for q in chunk]
+        if side == 1:
+            for i, q in enumerate(chunk):
+                core_add(main, q, far[0][i], 1 - y, 1 - x)
+                far_x.append(x_send(main, q, 1 - y))
         net_part(core, 1 - y, xt)
+    x_add(main, whole, own_x, y)
+    own_z = z_send(main, whole, y)
     w_z = []
     for block in (0, 1):
         x_add(weight, only, w_x[block], block)
@@ -390,18 +395,13 @@
     def chunk_steps(q, start, gap):
         state = {}
 
-        @step(0)
-        def _():
-            core_add(main, chunk[q], far[0][q], 1 - y, 1 - x)
-            state["x"] = x_send(main, chunk[q], 1 - y)
-
         @step(start + 0.5 * gap)
         def _():
             core_add(main, chunk[q], far[1][q], 1 - y, x)
 
         @step(start + gap)
         def _():
-            x_add(main, chunk[q], state["x"], 1 - y)
+            x_add(main, chunk[q], far_x[q], 1 - y)
             state["z"] = z_send(main, chunk[q], 1 - y)
 
         @step(start + 2 * gap)

time: 62.1 us -> 68.1 us (1.097)
  Pallas kernels: 58.8 us -> 64.8 us
    pallas_call x1, Pallas kernels: 58.8 us -> 64.8 us  [fused_shards(): pl.pallas_call(exchange_kernel, out_shape=(pltpu.VMEM((rows, width), BF16...]
where the time goes in v6:
time: 68.1 us; the launch traced here: 67.8 us
  Pallas kernels  64.8 us (95%)
  local copies, waits for them, and re-layouts  1.77 us (3%)
  between operations  1.29 us (2%)
    pallas_call x1, Pallas kernels, fused_shards(): pl.pallas_call(exchange_kernel, out_shape=(pltpu.VMEM((rows, width), BF16...  64.8 us
    unnamed x2, local copies, waits for them, and re-layouts  1.77 us

profile of v6, /device:TPU:0, one launch (start us, length us, event | category | flops | bytes accessed | tf_op | source)
XLA Modules:
  0.0 67.8 jit_solution(10764423158275549559)
XLA Ops:
  1.3 64.8 %shard_map.95 = (bf16[1024,512]{1,0:T(8,128)(2,1)S(1)}, bf16[512,512]{1,0:T(8,128)(2,1)S(1)}) custom-call(bf16[1024,512]{1,0:T(8,128)(2,1)} %grad_out.1, bf16[1024,512]{1,0:T(8,128)(2,1)} %saved_agg.1, bf16[512,512]{1,0:T(8,128)(2,1)} %theta.1, bf16[1,1,16,128,128]{4,3,2,1,0:T(8,128)(2,1)} %tile_values.1, s32[1,1,2,16]{3,2,1,0:T(2,128)} %bitcast.5, ...), custom_call_target="tpu_custom_call" | custom-call | tf_op jit(solution)/shard_map/pallas_call | solution.py:496
  66.1 1.0 %copy.12 = bf16[1024,512]{1,0:T(8,128)(2,1)} copy(bf16[1024,512]{1,0:T(8,128)(2,1)S(1)} %get-tuple-element.2) | data formatting | bytes 2097152
  67.1 0.8 %copy.13 = bf16[512,512]{1,0:T(8,128)(2,1)} copy(bf16[512,512]{1,0:T(8,128)(2,1)S(1)} %get-tuple-element.3) | data formatting | bytes 1048576

commit v7 on v6

--- a/solution.py
+++ b/solution.py
@@ -294,6 +294,9 @@
     for block in (0, 1):
         core_add(weight, only, w_core[block, 1], block, x)
 
+    x_add(main, whole, own_x, y)
+    own_z = z_send(main, whole, y)
+
     inv_copy.wait_recv()
     inv_move = pltpu.make_async_copy(inv_land, inv_far, local_sem.at[4])
     inv_move.start()
@@ -311,8 +314,6 @@
                 core_add(main, q, far[0][i], 1 - y, 1 - x)
                 far_x.append(x_send(main, q, 1 - y))
         net_part(core, 1 - y, xt)
-    x_add(main, whole, own_x, y)
-    own_z = z_send(main, whole, y)
     w_z = []
     for block in (0, 1):
         x_add(weight, only, w_x[block], block)

time: 68.1 us -> 63.4 us (0.931)
  Pallas kernels: 64.8 us -> 60.1 us
    pallas_call x1, Pallas kernels: 64.8 us -> 60.1 us  [fused_shards(): pl.pallas_call(exchange_kernel, out_shape=(pltpu.VMEM((rows, width), BF16...]
where the time goes in v7:
time: 63.4 us; the launch traced here: 63.2 us
  Pallas kernels  60.1 us (95%)
  local copies, waits for them, and re-layouts  1.77 us (3%)
  between operations  1.29 us (2%)
    pallas_call x1, Pallas kernels, fused_shards(): pl.pallas_call(exchange_kernel, out_shape=(pltpu.VMEM((rows, width), BF16...  60.1 us
    unnamed x2, local copies, waits for them, and re-layouts  1.77 us

profile of v7, /device:TPU:0, one launch (start us, length us, event | category | flops | bytes accessed | tf_op | source)
XLA Modules:
  0.0 63.2 jit_solution(15174571309199054349)
XLA Ops:
  1.3 60.1 %shard_map.95 = (bf16[1024,512]{1,0:T(8,128)(2,1)S(1)}, bf16[512,512]{1,0:T(8,128)(2,1)S(1)}) custom-call(bf16[1024,512]{1,0:T(8,128)(2,1)} %grad_out.1, bf16[1024,512]{1,0:T(8,128)(2,1)} %saved_agg.1, bf16[512,512]{1,0:T(8,128)(2,1)} %theta.1, bf16[1,1,16,128,128]{4,3,2,1,0:T(8,128)(2,1)} %tile_values.1, s32[1,1,2,16]{3,2,1,0:T(2,128)} %bitcast.5, ...), custom_call_target="tpu_custom_call" | custom-call | tf_op jit(solution)/shard_map/pallas_call | solution.py:497
  61.4 1.0 %copy.12 = bf16[1024,512]{1,0:T(8,128)(2,1)} copy(bf16[1024,512]{1,0:T(8,128)(2,1)S(1)} %get-tuple-element.2) | data formatting | bytes 2097152
  62.4 0.8 %copy.13 = bf16[512,512]{1,0:T(8,128)(2,1)} copy(bf16[512,512]{1,0:T(8,128)(2,1)S(1)} %get-tuple-element.3) | data formatting | bytes 1048576
